TPU v7x, 512 devices: a whole 4x8x8 slice. The times are simulated.
512 devices in a mesh: row: 16 (over y, z_hi), col: 32 (over x, z_lo, core).
Axes of the slice: x: 4, y: 8, z: 8 (z_hi: 2, z_lo: 4; z = z_hi * 4 + z_lo), core: 2. Of those that a mesh axis runs over, the one named last changes fastest.
Arguments:
- factor: bfloat16 [28672, 28672], P('row', 'col'), may hold values from -2 to 2, as said below
- gradient: float32 [28672, 2048], P(('row', 'col')), may hold values from -6 to 6
- starts: int32 [16], replicated, may hold values from 0 to 15, each once
Outputs:
- solved: float32 [28672, 2048], P(('row', 'col'))
Inputs may be any that keep to these rules, and one draw needn't show every extreme that they name: `factor`: tiles above the block diagonal are zero, and every diagonal tile is upper triangular. `starts`: every block column is the start of exactly one panel.
All inputs are finite; a program needn't handle non-finite values.
Results may differ from a plain program's by a relative error of at most 0.0046.
Values may be sent and summed in bfloat16 or wider, within the bound.
A program may use at most 64 MiB of HBM per device.

v0:
```python
import jax
import jax.numpy as jnp
from jax import lax
from jax.sharding import PartitionSpec as P

TICKS = 6


def partner(array, axis, bit):
    return lax.ppermute(array, axis, [(i, i ^ 1 << bit) for i in range(lax.axis_size(axis))])


def broadcast(value, axis, source):
    kept = jnp.where(lax.axis_index(axis) == source, value, 0).astype(value.dtype)
    return lax.psum(kept, axis)


def shifted(block, axis, distance):
    devices = range(lax.axis_size(axis))
    route = [((i - distance) % len(devices), i) for i in devices]
    return lax.ppermute(block, axis, route)


def body(factor, gradient, starts):
    row_count = gradient.shape[0]
    block_count = starts.shape[0]
    panel_width = gradient.shape[1] // block_count
    tile_rows = factor.shape[0]
    half_rows = factor.shape[1]
    col_count = lax.axis_size("col")
    row_idx = lax.axis_index("row")
    col_idx = lax.axis_index("col")
    block_col = col_idx // 2
    half_idx = col_idx % 2
    slots = jnp.arange(block_count, dtype=jnp.int32)
    start_hot = (starts[None, :] == slots[:, None]).astype(jnp.float32)
    pieces = gradient.reshape(2, row_count // 2, block_count, panel_width)
    ordered = jnp.einsum("jp,hrpw->jhrw", start_hot, pieces, precision=lax.Precision.HIGHEST)
    ordered = ordered.reshape(col_count * (row_count // 2), panel_width)
    received = lax.all_to_all(ordered, "col", split_axis=0, concat_axis=0, tiled=True)
    received = received.reshape(col_count, row_count // 2, panel_width)
    keep_first = (half_idx == 0).astype(jnp.float32)
    keep_second = 1.0 - keep_first
    buffer = jnp.stack([received * keep_first, received * keep_second], axis=1).reshape(
        tile_rows, panel_width
    )
    zeros_tile = jnp.zeros((tile_rows, panel_width), jnp.float32)
    for tick_idx in range(TICKS):
        active = block_col >= tick_idx
        on_diag = active & (row_idx == block_col)
        below_diag = active & (row_idx > block_col)
        summed = buffer + partner(buffer, "col", 0)
        rounded = summed.astype(jnp.bfloat16)
        solution = lax.dot_general(
            factor, rounded, (((0,), (0,)), ((), ())), preferred_element_type=jnp.float32
        )
        solution_bf = solution.astype(jnp.bfloat16)
        arrived = broadcast(solution_bf, "row", block_col)
        update = jnp.dot(factor, arrived, preferred_element_type=jnp.float32)
        placed = lax.dynamic_update_slice_in_dim(zeros_tile, solution, half_idx * half_rows, 0)
        buffer = jnp.where(on_diag, placed, jnp.where(below_diag, buffer - update, buffer))
        if tick_idx + 1 < TICKS:
            buffer = shifted(buffer, "col", 2)
    end_hot = (((starts + (TICKS - 1)) % block_count)[None, :] == slots[:, None]).astype(
        jnp.float32
    )
    returned = lax.all_to_all(buffer, "col", split_axis=0, concat_axis=0, tiled=True)
    slot_rows = returned.reshape(block_count, 2, row_count, panel_width).sum(axis=1)
    result = jnp.einsum("jp,jrw->rpw", end_hot, slot_rows, precision=lax.Precision.HIGHEST)
    return result.reshape(row_count, block_count * panel_width)


def solution(mesh):
    in_specs = (P("row", "col"), P(("row", "col"), None), P())
    out_specs = P(("row", "col"), None)
    return jax.shard_map(body, mesh=mesh, in_specs=in_specs, out_specs=out_specs, check_vma=False)
```

profile of v0, /device:TPU:1, one launch (start us, length us, event | category | flops | bytes accessed | tf_op | source)
XLA Modules:
  0.0 1403.5 jit_solution(1890911971000149336)
XLA Ops:
  10.2 11.3 all-to-all-start
  21.6 16.8 %all-to-all-done = f32[32,28,128]{2,1,0:T(8,128)} async-done(((f32[32,28,128]{2,1,0:T(8,128)}), f32[32,28,128]{2,1,0:T(8,128)}, u32[]{:S(2)}, u32[]{:S(2)}) %all-to-all-start) | async-done | bytes 458784 | tf_op jit(solution)/shard_map/all_to_all | solution.py:40
  45.1 2.6 collective-permute-done
  48.7 2.9 constant_dynamic-update-slice_fusion.5
  52.5 2.4 copy.13
  54.9 185.7 %all-reduce.7.cloned.1.call-done = bf16[896,128]{0,1:T(8,128)(2,1)} async-done(((bf16[896,128]{0,1:T(8,128)(2,1)}), bf16[896,128]{0,1:T(8,128)(2,1)}) %all-reduce.7.cloned.1.call-update) | async-done | bytes 229392 | tf_op jit(solution)/shard_map/psum | solution.py:15
  240.6 2.6 fusion.17
  245.4 15.9 %collective-permute-done.1 = f32[1792,128]{0,1:T(8,128)S(1)} collective-permute-done((f32[1792,128]{0,1:T(8,128)S(1)}, f32[1792,128]{0,1:T(8,128)S(1)}, u32[]{:S(2)}, u32[]{:S(2)}) %collective-permute-start.1) | collective-permute-done | bytes 917536 | tf_op jit(solution)/shard_map/ppermute | solution.py:21
  261.3 14.7 %collective-permute-start.2 = (f32[1792,128]{0,1:T(8,128)S(1)}, f32[1792,128]{0,1:T(8,128)S(1)}, u32[]{:S(2)}, u32[]{:S(2)}) collective-permute-start(f32[1792,128]{0,1:T(8,128)S(1)} %collective-permute-done.1), channel_id=1, source_target_pairs={{0,1},{1,0},{2,3},{3,2},{4,5},{5,4},{6,7},{7,6},{8,9},{9,8},{10,11... | collective-permute-start | bytes 2752520 | tf_op jit(solution)/shard_map/ppermute | solution.py:10
  281.4 180.4 %all-reduce.9.cloned.1.call-done = bf16[896,128]{0,1:T(8,128)(2,1)} async-done(((bf16[896,128]{0,1:T(8,128)(2,1)}), bf16[896,128]{0,1:T(8,128)(2,1)}) %all-reduce.9.cloned.1.call-update) | async-done | bytes 229392 | tf_op jit(solution)/shard_map/psum | solution.py:15
  461.7 2.3 fusion.14
  464.1 2.5 collective-permute-start.3
  466.5 15.6 %collective-permute-done.3 = f32[1792,128]{0,1:T(8,128)S(1)} collective-permute-done((f32[1792,128]{0,1:T(8,128)S(1)}, f32[1792,128]{0,1:T(8,128)S(1)}, u32[]{:S(2)}, u32[]{:S(2)}) %collective-permute-start.3) | collective-permute-done | bytes 917536 | tf_op jit(solution)/shard_map/ppermute | solution.py:21
  482.2 14.7 %collective-permute-start.4 = (f32[1792,128]{0,1:T(8,128)S(1)}, f32[1792,128]{0,1:T(8,128)S(1)}, u32[]{:S(2)}, u32[]{:S(2)}) collective-permute-start(f32[1792,128]{0,1:T(8,128)S(1)} %collective-permute-done.3), channel_id=1, source_target_pairs={{0,1},{1,0},{2,3},{3,2},{4,5},{5,4},{6,7},{7,6},{8,9},{9,8},{10,11... | collective-permute-start | bytes 2752520 | tf_op jit(solution)/shard_map/ppermute | solution.py:10
  502.3 180.6 %all-reduce.11.cloned.1.call-done = bf16[896,128]{0,1:T(8,128)(2,1)} async-done(((bf16[896,128]{0,1:T(8,128)(2,1)}), bf16[896,128]{0,1:T(8,128)(2,1)}) %all-reduce.11.cloned.1.call-update) | async-done | bytes 229392 | tf_op jit(solution)/shard_map/psum | solution.py:15
  685.2 2.5 collective-permute-start.5
  687.7 15.6 %collective-permute-done.5 = f32[1792,128]{0,1:T(8,128)S(1)} collective-permute-done((f32[1792,128]{0,1:T(8,128)S(1)}, f32[1792,128]{0,1:T(8,128)S(1)}, u32[]{:S(2)}, u32[]{:S(2)}) %collective-permute-start.5) | collective-permute-done | bytes 917536 | tf_op jit(solution)/shard_map/ppermute | solution.py:21
  703.3 14.7 %collective-permute-start.6 = (f32[1792,128]{0,1:T(8,128)S(1)}, f32[1792,128]{0,1:T(8,128)S(1)}, u32[]{:S(2)}, u32[]{:S(2)}) collective-permute-start(f32[1792,128]{0,1:T(8,128)S(1)} %collective-permute-done.5), channel_id=1, source_target_pairs={{0,1},{1,0},{2,3},{3,2},{4,5},{5,4},{6,7},{7,6},{8,9},{9,8},{10,11... | collective-permute-start | bytes 2752520 | tf_op jit(solution)/shard_map/ppermute | solution.py:10
  723.4 180.7 %all-reduce.13.cloned.1.call-done = bf16[896,128]{0,1:T(8,128)(2,1)} async-done(((bf16[896,128]{0,1:T(8,128)(2,1)}), bf16[896,128]{0,1:T(8,128)(2,1)}) %all-reduce.13.cloned.1.call-update) | async-done | bytes 229392 | tf_op jit(solution)/shard_map/psum | solution.py:15
  906.4 2.5 collective-permute-start.7
  908.9 15.6 %collective-permute-done.7 = f32[1792,128]{0,1:T(8,128)S(1)} collective-permute-done((f32[1792,128]{0,1:T(8,128)S(1)}, f32[1792,128]{0,1:T(8,128)S(1)}, u32[]{:S(2)}, u32[]{:S(2)}) %collective-permute-start.7) | collective-permute-done | bytes 917536 | tf_op jit(solution)/shard_map/ppermute | solution.py:21
  924.5 14.7 %collective-permute-start.8 = (f32[1792,128]{0,1:T(8,128)S(1)}, f32[1792,128]{0,1:T(8,128)S(1)}, u32[]{:S(2)}, u32[]{:S(2)}) collective-permute-start(f32[1792,128]{0,1:T(8,128)S(1)} %collective-permute-done.7), channel_id=1, source_target_pairs={{0,1},{1,0},{2,3},{3,2},{4,5},{5,4},{6,7},{7,6},{8,9},{9,8},{10,11... | collective-permute-start | bytes 2752520 | tf_op jit(solution)/shard_map/ppermute | solution.py:10
  944.6 180.7 %all-reduce.15.cloned.1.call-done = bf16[896,128]{0,1:T(8,128)(2,1)} async-done(((bf16[896,128]{0,1:T(8,128)(2,1)}), bf16[896,128]{0,1:T(8,128)(2,1)}) %all-reduce.15.cloned.1.call-update) | async-done | bytes 229392 | tf_op jit(solution)/shard_map/psum | solution.py:15
  1125.4 2.3 fusion.5
  1127.7 2.5 collective-permute-start.9
  1130.2 15.6 %collective-permute-done.9 = f32[1792,128]{0,1:T(8,128)S(1)} collective-permute-done((f32[1792,128]{0,1:T(8,128)S(1)}, f32[1792,128]{0,1:T(8,128)S(1)}, u32[]{:S(2)}, u32[]{:S(2)}) %collective-permute-start.9) | collective-permute-done | bytes 917536 | tf_op jit(solution)/shard_map/ppermute | solution.py:21
  1145.8 14.9 %collective-permute-start.10 = (f32[1792,128]{0,1:T(8,128)S(1)}, f32[1792,128]{0,1:T(8,128)S(1)}, u32[]{:S(2)}, u32[]{:S(2)}) collective-permute-start(f32[1792,128]{0,1:T(8,128)S(1)} %collective-permute-done.9), channel_id=1, source_target_pairs={{0,1},{1,0},{2,3},{3,2},{4,5},{5,4},{6,7},{7,6},{8,9},{9,8},{10,11... | collective-permute-start | bytes 2752520 | tf_op jit(solution)/shard_map/ppermute | solution.py:10
  1165.8 180.7 %all-reduce.17.cloned.1.call-done = bf16[896,128]{0,1:T(8,128)(2,1)} async-done(((bf16[896,128]{0,1:T(8,128)(2,1)}), bf16[896,128]{0,1:T(8,128)(2,1)}) %all-reduce.17.cloned.1.call-update) | async-done | bytes 229392 | tf_op jit(solution)/shard_map/psum | solution.py:15
  1346.6 3.3 fusion.2
  1349.8 2.4 copy.15
  1352.3 16.6 %all-to-all-start.1 = ((f32[32,56,128]{2,1,0:T(8,128)}), f32[32,56,128]{2,1,0:T(8,128)}, u32[]{:S(2)}, u32[]{:S(2)}) async-start(f32[32,56,128]{2,1,0:T(8,128)} %bitcast.103), calls=%async_computation.1 | async-start | bytes 1835008 | tf_op jit(solution)/shard_map/all_to_all | solution.py:67
  1369.0 25.1 %all-to-all-done.1 = f32[32,56,128]{2,1,0:T(8,128)} async-done(((f32[32,56,128]{2,1,0:T(8,128)}), f32[32,56,128]{2,1,0:T(8,128)}, u32[]{:S(2)}, u32[]{:S(2)}) %all-to-all-start.1) | async-done | bytes 917536 | tf_op jit(solution)/shard_map/all_to_all | solution.py:67
  (64 shorter events, 48.2 us)
Async XLA Ops:
  6.5 42.2 %copy-start = (bf16[1792,896]{1,0:T(8,128)(2,1)S(1)}, bf16[1792,896]{1,0:T(8,128)(2,1)}, u32[]{:S(2)}) copy-start(bf16[1792,896]{1,0:T(8,128)(2,1)} %param.3) | copy-start | bytes 9633796
  10.2 28.2 %all-to-all-start = ((f32[32,28,128]{2,1,0:T(8,128)}), f32[32,28,128]{2,1,0:T(8,128)}, u32[]{:S(2)}, u32[]{:S(2)}) async-start(f32[32,28,128]{2,1,0:T(8,128)} %copy.11), calls=%async_computation | async-start | bytes 1048576 | tf_op jit(solution)/shard_map/all_to_all | solution.py:40
  21.5 219.0 %all-reduce.7.cloned.1.call-start = ((), (), s32[]{:S(2)}) async-start(), calls=%async_computation.2 | async-start | bytes 458752 | tf_op jit(solution)/shard_map/psum | solution.py:15
  43.0 4.7 collective-permute-start
  52.4 409.4 %all-reduce.9.cloned.1.call-start = ((), (), s32[]{:S(2)}) async-start(), calls=%async_computation.3 | async-start | bytes 458752 | tf_op jit(solution)/shard_map/psum | solution.py:15
  243.2 18.1 %collective-permute-start.1 = (f32[1792,128]{0,1:T(8,128)S(1)}, f32[1792,128]{0,1:T(8,128)S(1)}, u32[]{:S(2)}, u32[]{:S(2)}) collective-permute-start(f32[1792,128]{0,1:T(8,128)S(1)} %fusion.17), channel_id=1, source_target_pairs={{30,0},{31,1},{0,2},{1,3},{2,4},{3,5},{4,6},{5,7},{6,8},{7,9},{8,1... | collective-permute-start | bytes 2752520 | tf_op jit(solution)/shard_map/ppermute | solution.py:21
  261.3 19.3 %copy-start.2 = (f32[1792,128]{0,1:T(8,128)}, f32[1792,128]{0,1:T(8,128)S(1)}, u32[]{:S(2)}) copy-start(f32[1792,128]{0,1:T(8,128)S(1)} %collective-permute-done.1) | copy-start | bytes 2752516
  261.3 16.8 %collective-permute-start.2 = (f32[1792,128]{0,1:T(8,128)S(1)}, f32[1792,128]{0,1:T(8,128)S(1)}, u32[]{:S(2)}, u32[]{:S(2)}) collective-permute-start(f32[1792,128]{0,1:T(8,128)S(1)} %collective-permute-done.1), channel_id=1, source_target_pairs={{0,1},{1,0},{2,3},{3,2},{4,5},{5,4},{6,7},{7,6},{8,9},{9,8},{10,11... | collective-permute-start | bytes 2752520 | tf_op jit(solution)/shard_map/ppermute | solution.py:10
  281.3 401.6 %all-reduce.11.cloned.1.call-start = ((), (), s32[]{:S(2)}) async-start(), calls=%async_computation.4 | async-start | bytes 458752 | tf_op jit(solution)/shard_map/psum | solution.py:15
  464.1 18.1 %collective-permute-start.3 = (f32[1792,128]{0,1:T(8,128)S(1)}, f32[1792,128]{0,1:T(8,128)S(1)}, u32[]{:S(2)}, u32[]{:S(2)}) collective-permute-start(f32[1792,128]{0,1:T(8,128)S(1)} %fusion.14), channel_id=1, source_target_pairs={{30,0},{31,1},{0,2},{1,3},{2,4},{3,5},{4,6},{5,7},{6,8},{7,9},{8,1... | collective-permute-start | bytes 2752520 | tf_op jit(solution)/shard_map/ppermute | solution.py:21
  482.2 19.3 %copy-start.3 = (f32[1792,128]{0,1:T(8,128)}, f32[1792,128]{0,1:T(8,128)S(1)}, u32[]{:S(2)}) copy-start(f32[1792,128]{0,1:T(8,128)S(1)} %collective-permute-done.3) | copy-start | bytes 2752516
  482.2 16.8 %collective-permute-start.4 = (f32[1792,128]{0,1:T(8,128)S(1)}, f32[1792,128]{0,1:T(8,128)S(1)}, u32[]{:S(2)}, u32[]{:S(2)}) collective-permute-start(f32[1792,128]{0,1:T(8,128)S(1)} %collective-permute-done.3), channel_id=1, source_target_pairs={{0,1},{1,0},{2,3},{3,2},{4,5},{5,4},{6,7},{7,6},{8,9},{9,8},{10,11... | collective-permute-start | bytes 2752520 | tf_op jit(solution)/shard_map/ppermute | solution.py:10
  502.2 401.9 %all-reduce.13.cloned.1.call-start = ((), (), s32[]{:S(2)}) async-start(), calls=%async_computation.5 | async-start | bytes 458752 | tf_op jit(solution)/shard_map/psum | solution.py:15
  685.2 18.1 %collective-permute-start.5 = (f32[1792,128]{0,1:T(8,128)S(1)}, f32[1792,128]{0,1:T(8,128)S(1)}, u32[]{:S(2)}, u32[]{:S(2)}) collective-permute-start(f32[1792,128]{0,1:T(8,128)S(1)} %fusion.11), channel_id=1, source_target_pairs={{30,0},{31,1},{0,2},{1,3},{2,4},{3,5},{4,6},{5,7},{6,8},{7,9},{8,1... | collective-permute-start | bytes 2752520 | tf_op jit(solution)/shard_map/ppermute | solution.py:21
  703.3 19.3 %copy-start.4 = (f32[1792,128]{0,1:T(8,128)}, f32[1792,128]{0,1:T(8,128)S(1)}, u32[]{:S(2)}) copy-start(f32[1792,128]{0,1:T(8,128)S(1)} %collective-permute-done.5) | copy-start | bytes 2752516
  703.3 16.8 %collective-permute-start.6 = (f32[1792,128]{0,1:T(8,128)S(1)}, f32[1792,128]{0,1:T(8,128)S(1)}, u32[]{:S(2)}, u32[]{:S(2)}) collective-permute-start(f32[1792,128]{0,1:T(8,128)S(1)} %collective-permute-done.5), channel_id=1, source_target_pairs={{0,1},{1,0},{2,3},{3,2},{4,5},{5,4},{6,7},{7,6},{8,9},{9,8},{10,11... | collective-permute-start | bytes 2752520 | tf_op jit(solution)/shard_map/ppermute | solution.py:10
  723.4 402.0 %all-reduce.15.cloned.1.call-start = ((), (), s32[]{:S(2)}) async-start(), calls=%async_computation.6 | async-start | bytes 458752 | tf_op jit(solution)/shard_map/psum | solution.py:15
  906.4 18.1 %collective-permute-start.7 = (f32[1792,128]{0,1:T(8,128)S(1)}, f32[1792,128]{0,1:T(8,128)S(1)}, u32[]{:S(2)}, u32[]{:S(2)}) collective-permute-start(f32[1792,128]{0,1:T(8,128)S(1)} %fusion.8), channel_id=1, source_target_pairs={{30,0},{31,1},{0,2},{1,3},{2,4},{3,5},{4,6},{5,7},{6,8},{7,9},{8,1... | collective-permute-start | bytes 2752520 | tf_op jit(solution)/shard_map/ppermute | solution.py:21
  924.5 19.3 %copy-start.5 = (f32[1792,128]{0,1:T(8,128)}, f32[1792,128]{0,1:T(8,128)S(1)}, u32[]{:S(2)}) copy-start(f32[1792,128]{0,1:T(8,128)S(1)} %collective-permute-done.7) | copy-start | bytes 2752516
  924.5 16.8 %collective-permute-start.8 = (f32[1792,128]{0,1:T(8,128)S(1)}, f32[1792,128]{0,1:T(8,128)S(1)}, u32[]{:S(2)}, u32[]{:S(2)}) collective-permute-start(f32[1792,128]{0,1:T(8,128)S(1)} %collective-permute-done.7), channel_id=1, source_target_pairs={{0,1},{1,0},{2,3},{3,2},{4,5},{5,4},{6,7},{7,6},{8,9},{9,8},{10,11... | collective-permute-start | bytes 2752520 | tf_op jit(solution)/shard_map/ppermute | solution.py:10
  944.6 402.0 %all-reduce.17.cloned.1.call-start = ((), (), s32[]{:S(2)}) async-start(), calls=%async_computation.7 | async-start | bytes 458752 | tf_op jit(solution)/shard_map/psum | solution.py:15
  1127.7 18.1 %collective-permute-start.9 = (f32[1792,128]{0,1:T(8,128)S(1)}, f32[1792,128]{0,1:T(8,128)S(1)}, u32[]{:S(2)}, u32[]{:S(2)}) collective-permute-start(f32[1792,128]{0,1:T(8,128)S(1)} %fusion.5), channel_id=1, source_target_pairs={{30,0},{31,1},{0,2},{1,3},{2,4},{3,5},{4,6},{5,7},{6,8},{7,9},{8,1... | collective-permute-start | bytes 2752520 | tf_op jit(solution)/shard_map/ppermute | solution.py:21
  1145.8 19.3 %copy-start.1 = (f32[1792,128]{0,1:T(8,128)}, f32[1792,128]{0,1:T(8,128)S(1)}, u32[]{:S(2)}) copy-start(f32[1792,128]{0,1:T(8,128)S(1)} %collective-permute-done.9) | copy-start | bytes 2752516
  1145.8 16.8 %collective-permute-start.10 = (f32[1792,128]{0,1:T(8,128)S(1)}, f32[1792,128]{0,1:T(8,128)S(1)}, u32[]{:S(2)}, u32[]{:S(2)}) collective-permute-start(f32[1792,128]{0,1:T(8,128)S(1)} %collective-permute-done.9), channel_id=1, source_target_pairs={{0,1},{1,0},{2,3},{3,2},{4,5},{5,4},{6,7},{7,6},{8,9},{9,8},{10,11... | collective-permute-start | bytes 2752520 | tf_op jit(solution)/shard_map/ppermute | solution.py:10
  1349.8 19.1 %copy-start.6 = (s32[16]{0:T(128)S(1)}, s32[16]{0:T(128)}, u32[]{:S(2)}) copy-start(s32[16]{0:T(128)} %param.5) | copy-start | bytes 196
  1352.3 41.8 %all-to-all-start.1 = ((f32[32,56,128]{2,1,0:T(8,128)}), f32[32,56,128]{2,1,0:T(8,128)}, u32[]{:S(2)}, u32[]{:S(2)}) async-start(f32[32,56,128]{2,1,0:T(8,128)} %bitcast.103), calls=%async_computation.1 | async-start | bytes 1835008 | tf_op jit(solution)/shard_map/all_to_all | solution.py:67
Sparse Core Ops, SparseCore 0:
  52.5 188.0 all-reduce.6
  281.4 180.2 all-reduce.8
  502.3 180.5 all-reduce.10
  723.5 180.5 all-reduce.12
  944.7 180.6 all-reduce.14
  1165.9 180.5 all-reduce.16
where the time goes:
time: 1400 us
  waiting for transfers between devices  1220 us (87%)
  starting transfers between devices  116 us (8%)
  matrix products  27.1 us (2%)
  local copies, waits for them, and re-layouts  17.9 us (1%)
    psum x6, waiting for transfers between devices, broadcast(): return lax.psum(kept, axis)  1090 us
    ppermute x5, waiting for transfers between devices, shifted(): return lax.ppermute(block, axis, route)  78.4 us
    ppermute x6, starting transfers between devices, partner(): lax.ppermute(array, axis, [(i, i ^ 1 << bit) for i in range(lax.axis_size...  75.6 us
  transfers between devices with their start and end apart: 19, of which 19 were waited for; matrix products, arithmetic and copies ran while one was open for 0% of the time, Pallas kernels for 0%

commit v1 on v0

v1 whole, which is shorter than its diff:
```python
import functools
import jax
import jax.numpy as jnp
from jax import lax
from jax.experimental import pallas as pl
from jax.experimental.pallas import tpu as pltpu
from jax.sharding import PartitionSpec as P

TICKS = 6
CHUNKS = 2
MESH = pl.DeviceIdType.MESH
F32 = jnp.float32
BF16 = jnp.bfloat16


def kernel(
    blocks, starts_ref, grad_ref, factor_ref, out_ref,
    tile, raw, diag, vec, res, solved, partial, sums, tail, grad_given, grad_own, grad_send, grad_in, x_ret, x_in, tail_in,
    load_sem, tile_sem, us_sem, u_sem, gs_sem, g_sem, vs_sem, v_sem, xs_sem, qs_sem, q_sem,
    ss_sem, s_sem, rs_sem, r_sem, ts_sem, t_sem,
):
    row = lax.axis_index("row")
    col = lax.axis_index("col")
    blk = col // 2
    half = col % 2
    owners = blocks
    rows = grad_ref.shape[0]
    width = grad_ref.shape[1] // blocks
    half_rows = factor_ref.shape[1]
    step = half_rows // CHUNKS
    group = owners // CHUNKS
    lanes = 128
    per = half_rows // lanes
    sib = col + 1 - 2 * half
    other = 1 - half
    is_diag = row == blk
    is_next = row == blk + 1
    is_lower = row > blk
    my_group = col // owners
    diag_core = 2 * row + my_group
    next_core = jnp.where(row > 0, diag_core - 2, diag_core)

    own_rows = pl.ds(pl.multiple_of(half * half_rows, half_rows), half_rows)
    other_rows = pl.ds(pl.multiple_of(other * half_rows, half_rows), half_rows)
    load_raw = pltpu.make_async_copy(factor_ref, raw, load_sem)
    load_half = pltpu.make_async_copy(factor_ref.at[own_rows], tile.at[half], load_sem)

    @pl.when(is_diag)
    def _():
        load_raw.start()

    @pl.when(is_lower)
    def _():
        load_half.start()

    barrier = pltpu.get_barrier_semaphore()

    @pl.loop(0, 2 * blocks)
    def _(c):
        @pl.when(c != col)
        def _():
            pl.semaphore_signal(barrier, inc=1, device_id=(row, c), device_id_type=MESH)

    far = [(1, 0), (2, 0), (-1, 0), (-2, 0), (1, 2), (2, 2), (-1, -2), (-2, -2)]
    for dr, dc in far:
        pl.semaphore_signal(
            barrier, inc=1, device_id=((row + dr + blocks) % blocks, (col + dc + 2 * blocks) % (2 * blocks)),
            device_id_type=MESH,
        )

    for p in range(blocks):
        grad_given[p] = grad_ref[:, p * width:(p + 1) * width]
    for s in range(blocks):
        which = jnp.int32(0)
        for p in range(blocks):
            which = which + jnp.where(starts_ref[p] == s, p, 0)
        grad_own[s] = grad_given[jnp.minimum(which, blocks - 1)]
    pad = jnp.zeros((64 - rows, width), F32)

    @pl.loop(0, TICKS)
    def _(t):
        @pl.when(row >= t)
        def _():
            grad_send[t] = jnp.concatenate([grad_own[row - t], pad], axis=0).astype(BF16)

        @pl.when(row < t)
        def _():
            grad_send[t] = jnp.zeros((64, width), BF16)

    pl.semaphore_wait(barrier, 2 * blocks - 1 + len(far))

    my_slot = col % owners
    pieces = ((0, 1, diag_core), (1, TICKS - 1, next_core))

    def grad_copy(k):
        lo, n, target = pieces[k]
        return pltpu.make_async_remote_copy(
            src_ref=grad_send.at[pl.ds(lo, n)],
            dst_ref=grad_in.at[pl.ds(lo, n), my_slot],
            send_sem=gs_sem.at[k], recv_sem=g_sem.at[k],
            device_id=(row, target), device_id_type=MESH,
        )

    def grad_local(k):
        lo, n, target = pieces[k]
        return pltpu.make_async_copy(
            grad_send.at[pl.ds(lo, n)], grad_in.at[pl.ds(lo, n), my_slot], g_sem.at[k]
        )

    def wait_grad(k):
        lo, n, target = pieces[k]
        pltpu.make_async_copy(grad_in.at[pl.ds(lo, n)], grad_in.at[pl.ds(lo, n)], g_sem.at[k]).wait()

    grad_goes = (row >= 0, row > 0)
    for k in range(2):
        @pl.when(grad_goes[k] & (col != pieces[k][2]))
        def _():
            grad_copy(k).start()

        @pl.when(grad_goes[k] & (col == pieces[k][2]))
        def _():
            grad_local(k).start()

    def diag_copy(h, k):
        part = (pl.ds(0, h * half_rows + (k + 1) * lanes), pl.ds(k * lanes, lanes))
        return pltpu.make_async_remote_copy(
            src_ref=factor_ref.at[part], dst_ref=raw.at[part],
            send_sem=us_sem.at[k], recv_sem=u_sem.at[k],
            device_id=(row, (col - 2 + 2 * blocks) % (2 * blocks)), device_id_type=MESH,
        )

    for h in range(2):
        @pl.when(is_diag & (row > 0) & (half == h))
        def _():
            for k in range(per):
                diag_copy(h, k).start()

    tile_copy = pltpu.make_async_remote_copy(
        src_ref=factor_ref.at[other_rows], dst_ref=tile.at[half],
        send_sem=tile_sem.at[0], recv_sem=tile_sem.at[1],
        device_id=(row, sib), device_id_type=MESH,
    )

    @pl.when(is_lower)
    def _():
        tile_copy.start()

    def lay_diag(k):
        m = slice(k * lanes, (k + 1) * lanes)

        @pl.loop(0, 2 * per)
        def _(n):
            src = pl.ds(pl.multiple_of(n * lanes, lanes), lanes)
            dst = pl.ds(pl.multiple_of((n % per) * lanes, lanes), lanes)

            @pl.when(n <= half * per + k)
            def _():
                diag[n // per, m, dst] = raw[src, m].T

            @pl.when(n > half * per + k)
            def _():
                diag[n // per, m, dst] = jnp.zeros((lanes, lanes), BF16)

    def chunk(m):
        return pl.ds(pl.multiple_of(m * step, step), step)

    def sibling_copy(ref, t, m, send_sem, recv_sem):
        part = ref.at[t, half, chunk(m)]
        return pltpu.make_async_remote_copy(
            src_ref=part, dst_ref=part, send_sem=send_sem.at[t, m], recv_sem=recv_sem.at[t, m],
            device_id=(row, sib), device_id_type=MESH,
        )

    def vec_copy(t, m):
        return sibling_copy(vec, t, m, vs_sem.at[0], v_sem.at[0])

    def res_copy(t, m):
        return sibling_copy(res, t, m, qs_sem, q_sem)

    def forward_copy(t, m):
        part = vec.at[t, half, chunk(m)]
        return pltpu.make_async_remote_copy(
            src_ref=part, dst_ref=part, send_sem=vs_sem.at[1, t, m], recv_sem=v_sem.at[1, t, m],
            device_id=((row + 2) % blocks, col), device_id_type=MESH,
        )

    def solved_copy(t, m, k):
        return pltpu.make_async_remote_copy(
            src_ref=solved.at[t, chunk(m)], dst_ref=vec.at[t, half, chunk(m)],
            send_sem=xs_sem.at[k - 1, t, m], recv_sem=v_sem.at[1, t, m],
            device_id=((row + k) % blocks, 2 * row + half), device_id_type=MESH,
        )

    def partial_copy(t, m):
        return pltpu.make_async_remote_copy(
            src_ref=sums.at[t, chunk(m)], dst_ref=partial.at[(t + 1) % TICKS, chunk(m)],
            send_sem=ss_sem.at[t, m], recv_sem=s_sem.at[(t + 1) % TICKS, m],
            device_id=(row, (col + 2) % (2 * blocks)), device_id_type=MESH,
        )

    def wait_partial(t, m):
        pltpu.make_async_copy(partial.at[t, chunk(m)], partial.at[t, chunk(m)], s_sem.at[t, m]).wait()

    padding = jnp.zeros((group, 64 - rows, width), F32)

    def laid(y):
        return jnp.concatenate([y.reshape(group, rows, width), padding], axis=1).astype(BF16)

    def given(t, m):
        return grad_in[t, m * group:(m + 1) * group].astype(F32)[:, :rows].reshape(step, width)

    def solve(t):
        for m in range(CHUNKS):
            res_copy(t, m).wait_recv()
        for m in range(CHUNKS):
            x = jnp.dot(diag[0, chunk(m)], res[t, 0], preferred_element_type=F32)
            x = x + jnp.dot(diag[1, chunk(m)], res[t, 1], preferred_element_type=F32)
            solved[t, chunk(m)] = x.astype(BF16)
            for k in (1, 2):
                @pl.when(row + k < blocks)
                def _():
                    solved_copy(t, m, k).start()
            x_ret[t, m * group:(m + 1) * group] = laid(x)

    @pl.when(is_diag)
    def _():
        load_raw.wait()
        for k in range(per):
            lay_diag(k)
        wait_grad(0)
        for m in range(CHUNKS):
            res[0, half, chunk(m)] = given(0, m).astype(BF16)
            res_copy(0, m).start()
        solve(0)

    @pl.when(is_lower)
    def _():
        load_half.wait()
        tile_copy.wait_recv()

    def give(o, src, dst, send_sem, recv_sem):
        target = half * owners + o

        @pl.when(target != col)
        def _():
            pltpu.make_async_remote_copy(
                src_ref=src, dst_ref=dst, send_sem=send_sem, recv_sem=recv_sem,
                device_id=(row, target), device_id_type=MESH,
            ).start()

        @pl.when(target == col)
        def _():
            pltpu.make_async_copy(src, dst, recv_sem).start()

    slot = jnp.clip(blk - (TICKS - 1), 0, tail_in.shape[0] - 1)
    rest = pl.ds(1, TICKS - 1)

    @pl.when(is_diag)
    def _():
        @pl.loop(0, owners)
        def _(o):
            give(o, x_ret.at[0, o], x_in.at[0], rs_sem, r_sem.at[0])

    def tick(t):
        for m in range(CHUNKS):
            solved_copy(t, m, 1).wait_recv()

            @pl.when(row + 2 < blocks)
            def _():
                forward_copy(t, m).start()

            vec_copy(t, m).start()

        for m in range(CHUNKS):
            vec_copy(t, m).wait_recv()

        @pl.when(is_next & (t == 0))
        def _():
            wait_grad(1)

        for m in range(CHUNKS):
            y = jnp.dot(tile[0, chunk(m)], vec[t, 0], preferred_element_type=F32)
            y = y + jnp.dot(tile[1, chunk(m)], vec[t, 1], preferred_element_type=F32)
            sums[t, chunk(m)] = y

            @pl.when(t > 0)
            def _():
                wait_partial(t, m)
                sums[t, chunk(m)] = sums[t, chunk(m)] + partial[t, chunk(m)]

            @pl.when(t == TICKS - 1)
            def _():
                tail[m * group:(m + 1) * group] = laid(sums[t, chunk(m)])

            @pl.when((t < TICKS - 1) & jnp.logical_not(is_next))
            def _():
                partial_copy(t, m).start()

            @pl.when((t < TICKS - 1) & is_next)
            def _():
                after = jnp.minimum(t + 1, TICKS - 1)
                res[after, half, chunk(m)] = (given(after, m) - sums[t, chunk(m)]).astype(BF16)
                res_copy(after, m).start()

        @pl.when(is_next & (t < TICKS - 1))
        def _():
            @pl.when(t == 0)
            def _():
                for k in range(per):
                    for h in range(2):
                        @pl.when(half == h)
                        def _():
                            diag_copy(h, k).wait_recv()
                    lay_diag(k)

            solve(jnp.minimum(t + 1, TICKS - 1))

    @pl.loop(0, TICKS)
    def _(t):
        @pl.when(is_next & (t == TICKS - 1))
        def _():
            @pl.loop(0, owners)
            def _(o):
                give(o, x_ret.at[rest, o], x_in.at[rest], rs_sem, r_sem.at[1])

        @pl.when(is_lower & (blk >= t))
        def _():
            tick(t)

    has_tail = is_lower & (blk >= TICKS - 1)

    @pl.when(has_tail)
    def _():
        @pl.loop(0, owners)
        def _(o):
            give(o, tail.at[o], tail_in.at[slot], ts_sem, t_sem.at[slot])

    pltpu.make_async_copy(x_in.at[0], x_in.at[0], r_sem.at[0]).wait()

    @pl.when(row > 0)
    def _():
        pltpu.make_async_copy(x_in.at[rest], x_in.at[rest], r_sem.at[1]).wait()

    @pl.loop(0, blocks)
    def _(s):
        t = row - s

        @pl.when((t >= 0) & (t < TICKS))
        def _():
            grad_own[s] = x_in[jnp.clip(t, 0, TICKS - 1)].astype(F32)[:rows]

        @pl.when(t >= TICKS)
        def _():
            ref = tail_in.at[jnp.minimum(s, tail_in.shape[0] - 1)]
            pltpu.make_async_copy(ref, ref, t_sem.at[jnp.minimum(s, tail_in.shape[0] - 1)]).wait()
            grad_own[s] = grad_own[s] - ref[...].astype(F32)[:rows]

    for p in range(blocks):
        out_ref[:, p * width:(p + 1) * width] = grad_own[starts_ref[p]]

    for k in range(2):
        @pl.when(grad_goes[k] & (col != pieces[k][2]))
        def _():
            grad_copy(k).wait_send()

    for h in range(2):
        @pl.when(is_diag & (row > 0) & (half == h))
        def _():
            for k in range(per):
                diag_copy(h, k).wait_send()

    @pl.when(is_lower)
    def _():
        tile_copy.wait_send()

    @pl.loop(0, TICKS)
    def _(t):
        for m in range(CHUNKS):
            @pl.when((is_diag & (t == 0)) | (is_next & (t > 0) & (row >= t)))
            def _():
                res_copy(t, m).wait_send()
                for k in (1, 2):
                    @pl.when(row + k < blocks)
                    def _():
                        solved_copy(t, m, k).wait_send()

            @pl.when(is_lower & (blk >= t))
            def _():
                vec_copy(t, m).wait_send()

                @pl.when(row + 2 < blocks)
                def _():
                    forward_copy(t, m).wait_send()

                @pl.when((t < TICKS - 1) & jnp.logical_not(is_next))
                def _():
                    partial_copy(t, m).wait_send()

    def sent_all(ref_all, ref_less, sem):
        @pl.when(my_group == half)
        def _():
            pltpu.make_async_copy(ref_less, ref_less, sem).wait()

        @pl.when(my_group != half)
        def _():
            pltpu.make_async_copy(ref_all, ref_all, sem).wait()

    less = pl.ds(0, owners - 1)

    @pl.when(has_tail)
    def _():
        sent_all(tail, tail.at[less], ts_sem)

    @pl.when(is_diag)
    def _():
        sent_all(x_ret.at[0], x_ret.at[0, less], rs_sem)

    @pl.when(is_next)
    def _():
        sent_all(x_ret.at[rest], x_ret.at[rest, less], rs_sem)


def body(factor, gradient, starts):
    blocks = starts.shape[0]
    rows = gradient.shape[0]
    width = gradient.shape[1] // blocks
    tile_rows, half_rows = factor.shape
    owners = blocks
    vmem = pltpu.VMEM
    dma = pltpu.SemaphoreType.DMA
    spare = max(blocks - TICKS, 1)
    scratch = [
        vmem((2, half_rows, half_rows), BF16),
        vmem((tile_rows, half_rows), BF16),
        vmem((2, half_rows, half_rows), BF16),
        vmem((TICKS, 2, half_rows, width), BF16),
        vmem((TICKS, 2, half_rows, width), BF16),
        vmem((TICKS, half_rows, width), BF16),
        vmem((TICKS, half_rows, width), F32),
        vmem((TICKS, half_rows, width), F32),
        vmem((owners, 64, width), BF16),
        vmem((blocks, rows, width), F32),
        vmem((blocks, rows, width), F32),
        vmem((TICKS, 64, width), BF16),
        vmem((TICKS, owners, 64, width), BF16),
        vmem((TICKS, owners, 64, width), BF16),
        vmem((TICKS, 64, width), BF16),
        vmem((spare, 64, width), BF16),
        dma, dma((2,)), dma((half_rows // 128,)), dma((half_rows // 128,)), dma((2,)), dma((2,)),
        dma((2, TICKS, CHUNKS)), dma((2, TICKS, CHUNKS)), dma((2, TICKS, CHUNKS)),
        dma((TICKS, CHUNKS)), dma((TICKS, CHUNKS)), dma((TICKS, CHUNKS)), dma((TICKS, CHUNKS)),
        dma, dma((2,)), dma, dma((spare,)),
    ]
    return pl.pallas_call(
        functools.partial(kernel, blocks),
        out_shape=jax.ShapeDtypeStruct(gradient.shape, F32),
        in_specs=[
            pl.BlockSpec(memory_space=pltpu.SMEM),
            pl.BlockSpec(memory_space=pltpu.VMEM),
            pl.BlockSpec(memory_space=pl.ANY),
        ],
        out_specs=pl.BlockSpec(memory_space=pltpu.VMEM),
        scratch_shapes=scratch,
        compiler_params=pltpu.CompilerParams(
            collective_id=0, has_side_effects=True, vmem_limit_bytes=62 * 1024 * 1024
        ),
        cost_estimate=pl.CostEstimate(
            flops=2 * TICKS * tile_rows * half_rows * width,
            bytes_accessed=2 * tile_rows * half_rows, transcendentals=0,
        ),
    )(starts, gradient, factor)


def solution(mesh):
    in_specs = (P("row", "col"), P(("row", "col"), None), P())
    out_specs = P(("row", "col"), None)
    return jax.shard_map(body, mesh=mesh, in_specs=in_specs, out_specs=out_specs, check_vma=False)
```

time: 1400 us -> 173 us (0.12)
  the two profiles are of different devices: /device:TPU:1 before, /device:TPU:51 now
where the time goes in v1:
time: 173 us
  Pallas kernels  171 us (99%)
  local copies, waits for them, and re-layouts  1.82 us (1%)
    pallas_call x1, Pallas kernels, body(): pl.pallas_call(functools.partial(kernel, blocks), out_shape=jax.ShapeDtyp...  171 us

profile of v1, /device:TPU:51, one launch (start us, length us, event | category | flops | bytes accessed | tf_op | source)
XLA Modules:
  0.0 172.7 jit_solution(18403487722753669242)
XLA Ops:
  0.0 170.9 %shard_map.37 = f32[56,2048]{1,0:T(8,128)} custom-call(s32[16]{0:T(128)} %starts_ref.1, f32[56,2048]{1,0:T(8,128)} %grad_ref.1, bf16[1792,896]{1,0:T(8,128)(2,1)} %factor_ref.1), custom_call_target="tpu_custom_call" | custom-call | flops 2466250752 | bytes 3211264 | tf_op jit(solution)/shard_map/pallas_call | solution.py:454
  170.9 1.8 %copy.5 = f32[56,2048]{1,0:T(8,128)} copy(f32[56,2048]{1,0:T(8,128)} %shard_map.37) | data formatting | bytes 917504

commit v2 on v1

--- a/solution.py
+++ b/solution.py
@@ -15,9 +15,10 @@
 
 def kernel(
     blocks, starts_ref, grad_ref, factor_ref, out_ref,
-    tile, raw, diag, vec, res, solved, partial, sums, tail, grad_given, grad_own, grad_send, grad_in, x_ret, x_in, tail_in,
+    tile, raw, diag, vec, res, solved, partial, sums, near, near_sums, first, first_in,
+    tail, grad_given, grad_own, grad_send, grad_in, x_ret, x_in, tail_in,
     load_sem, tile_sem, us_sem, u_sem, gs_sem, g_sem, vs_sem, v_sem, xs_sem, qs_sem, q_sem,
-    ss_sem, s_sem, rs_sem, r_sem, ts_sem, t_sem,
+    ss_sem, s_sem, fs_sem, f_sem, rs_sem, r_sem, ts_sem, t_sem,
 ):
     row = lax.axis_index("row")
     col = lax.axis_index("col")
@@ -36,6 +37,9 @@
     is_diag = row == blk
     is_next = row == blk + 1
     is_lower = row > blk
+    is_upper = row < blk
+    apart = row % 4 == 0
+    moved = jnp.logical_not(apart)
     my_group = col // owners
     diag_core = 2 * row + my_group
     next_core = jnp.where(row > 0, diag_core - 2, diag_core)
@@ -90,7 +94,7 @@
     pl.semaphore_wait(barrier, 2 * blocks - 1 + len(far))
 
     my_slot = col % owners
-    pieces = ((0, 1, diag_core), (1, TICKS - 1, next_core))
+    pieces = ((0, 1, diag_core), (1, 1, diag_core), (2, TICKS - 2, jnp.where(apart, diag_core, next_core)))
 
     def grad_copy(k):
         lo, n, target = pieces[k]
@@ -111,15 +115,21 @@
         lo, n, target = pieces[k]
         pltpu.make_async_copy(grad_in.at[pl.ds(lo, n)], grad_in.at[pl.ds(lo, n)], g_sem.at[k]).wait()
 
-    grad_goes = (row >= 0, row > 0)
-    for k in range(2):
-        @pl.when(grad_goes[k] & (col != pieces[k][2]))
+    def send_grad(k):
+        @pl.when(col != pieces[k][2])
         def _():
             grad_copy(k).start()
 
-        @pl.when(grad_goes[k] & (col == pieces[k][2]))
+        @pl.when(col == pieces[k][2])
         def _():
             grad_local(k).start()
+
+    send_grad(0)
+    send_grad(1)
+
+    @pl.when(row > 0)
+    def _():
+        send_grad(2)
 
     def diag_copy(h, k):
         part = (pl.ds(0, h * half_rows + (k + 1) * lanes), pl.ds(k * lanes, lanes))
@@ -130,7 +140,7 @@
         )
 
     for h in range(2):
-        @pl.when(is_diag & (row > 0) & (half == h))
+        @pl.when(is_diag & moved & (half == h))
         def _():
             for k in range(per):
                 diag_copy(h, k).start()
@@ -187,19 +197,34 @@
     def solved_copy(t, m, k):
         return pltpu.make_async_remote_copy(
             src_ref=solved.at[t, chunk(m)], dst_ref=vec.at[t, half, chunk(m)],
-            send_sem=xs_sem.at[k - 1, t, m], recv_sem=v_sem.at[1, t, m],
-            device_id=((row + k) % blocks, 2 * row + half), device_id_type=MESH,
-        )
-
-    def partial_copy(t, m):
-        return pltpu.make_async_remote_copy(
-            src_ref=sums.at[t, chunk(m)], dst_ref=partial.at[(t + 1) % TICKS, chunk(m)],
-            send_sem=ss_sem.at[t, m], recv_sem=s_sem.at[(t + 1) % TICKS, m],
-            device_id=(row, (col + 2) % (2 * blocks)), device_id_type=MESH,
-        )
-
-    def wait_partial(t, m):
-        pltpu.make_async_copy(partial.at[t, chunk(m)], partial.at[t, chunk(m)], s_sem.at[t, m]).wait()
+            send_sem=xs_sem.at[k, t, m], recv_sem=v_sem.at[1, t, m],
+            device_id=((row + 1 + k) % blocks, 2 * row + half), device_id_type=MESH,
+        )
+
+    into_next = row == blk + 2
+    right = (row, (col + 2) % (2 * blocks))
+
+    def partial_copy(t, m, src, dst, k):
+        return pltpu.make_async_remote_copy(
+            src_ref=src.at[t, chunk(m)], dst_ref=dst.at[(t + 1) % TICKS, chunk(m)],
+            send_sem=ss_sem.at[k, t, m], recv_sem=s_sem.at[k, (t + 1) % TICKS, m],
+            device_id=right, device_id_type=MESH,
+        )
+
+    def far_sum(t, m):
+        return partial_copy(t, m, sums, partial, 0)
+
+    def near_sum(t, m):
+        return partial_copy(t, m, near_sums, near, 1)
+
+    def wait_sum(ref, t, m, k):
+        pltpu.make_async_copy(ref.at[t, chunk(m)], ref.at[t, chunk(m)], s_sem.at[k, t, m]).wait()
+
+    def first_copy(t, m):
+        return pltpu.make_async_remote_copy(
+            src_ref=first.at[t, chunk(m)], dst_ref=first_in.at[t, chunk(m)],
+            send_sem=fs_sem.at[t, m], recv_sem=f_sem.at[t, m], device_id=right, device_id_type=MESH,
+        )
 
     padding = jnp.zeros((group, 64 - rows, width), F32)
 
@@ -216,11 +241,41 @@
             x = jnp.dot(diag[0, chunk(m)], res[t, 0], preferred_element_type=F32)
             x = x + jnp.dot(diag[1, chunk(m)], res[t, 1], preferred_element_type=F32)
             solved[t, chunk(m)] = x.astype(BF16)
-            for k in (1, 2):
-                @pl.when(row + k < blocks)
+            for k in range(2):
+                @pl.when(row + 1 + k < blocks)
                 def _():
                     solved_copy(t, m, k).start()
             x_ret[t, m * group:(m + 1) * group] = laid(x)
+
+    def give(o, src, dst, send_sem, recv_sem):
+        target = half * owners + o
+
+        @pl.when(target != col)
+        def _():
+            pltpu.make_async_remote_copy(
+                src_ref=src, dst_ref=dst, send_sem=send_sem, recv_sem=recv_sem,
+                device_id=(row, target), device_id_type=MESH,
+            ).start()
+
+        @pl.when(target == col)
+        def _():
+            pltpu.make_async_copy(src, dst, recv_sem).start()
+
+    slot = jnp.clip(blk - (TICKS - 1), 0, tail_in.shape[0] - 1)
+    start = pl.ds(0, 2)
+    rest = pl.ds(2, TICKS - 2)
+
+    def give_rest():
+        @pl.loop(0, owners)
+        def _(o):
+            give(o, x_ret.at[rest, o], x_in.at[rest], rs_sem.at[1], r_sem.at[1])
+
+    def solve_apart(t):
+        for m in range(CHUNKS):
+            first_copy(t, m).wait_recv()
+            res[t, half, chunk(m)] = (given(t, m) - first_in[t, chunk(m)].astype(F32)).astype(BF16)
+            res_copy(t, m).start()
+        solve(t)
 
     @pl.when(is_diag)
     def _():
@@ -232,38 +287,57 @@
             res[0, half, chunk(m)] = given(0, m).astype(BF16)
             res_copy(0, m).start()
         solve(0)
+        wait_grad(1)
+
+        @pl.when(row > 0)
+        def _():
+            solve_apart(1)
+
+        @pl.loop(0, owners)
+        def _(o):
+            give(o, x_ret.at[start, o], x_in.at[start], rs_sem.at[0], r_sem.at[0])
+
+        @pl.when(apart & (row > 0))
+        def _():
+            wait_grad(2)
+
+            @pl.loop(2, TICKS)
+            def _(t):
+                @pl.when(row >= t)
+                def _():
+                    solve_apart(t)
+
+            give_rest()
 
     @pl.when(is_lower)
     def _():
+        partial[0] = jnp.zeros_like(partial[0])
+        near[0] = jnp.zeros_like(near[0])
         load_half.wait()
         tile_copy.wait_recv()
 
-    def give(o, src, dst, send_sem, recv_sem):
-        target = half * owners + o
-
-        @pl.when(target != col)
-        def _():
-            pltpu.make_async_remote_copy(
-                src_ref=src, dst_ref=dst, send_sem=send_sem, recv_sem=recv_sem,
-                device_id=(row, target), device_id_type=MESH,
-            ).start()
-
-        @pl.when(target == col)
-        def _():
-            pltpu.make_async_copy(src, dst, recv_sem).start()
-
-    slot = jnp.clip(blk - (TICKS - 1), 0, tail_in.shape[0] - 1)
-    rest = pl.ds(1, TICKS - 1)
-
-    @pl.when(is_diag)
-    def _():
-        @pl.loop(0, owners)
-        def _(o):
-            give(o, x_ret.at[0, o], x_in.at[0], rs_sem, r_sem.at[0])
+    def wait_start():
+        pltpu.make_async_copy(x_in.at[start], x_in.at[start], r_sem.at[0]).wait()
+
+    @pl.when(is_upper)
+    def _():
+        wait_start()
+
+    def lay_blocks(lo, hi):
+        for k in range(lo, hi):
+            for h in range(2):
+                @pl.when(half == h)
+                def _():
+                    diag_copy(h, k).wait_recv()
+            lay_diag(k)
+
+    def product(t, m):
+        y = jnp.dot(tile[0, chunk(m)], vec[t, 0], preferred_element_type=F32)
+        return y + jnp.dot(tile[1, chunk(m)], vec[t, 1], preferred_element_type=F32)
 
     def tick(t):
         for m in range(CHUNKS):
-            solved_copy(t, m, 1).wait_recv()
+            forward_copy(t, m).wait_recv()
 
             @pl.when(row + 2 < blocks)
             def _():
@@ -274,54 +348,75 @@
         for m in range(CHUNKS):
             vec_copy(t, m).wait_recv()
 
-        @pl.when(is_next & (t == 0))
-        def _():
-            wait_grad(1)
-
-        for m in range(CHUNKS):
-            y = jnp.dot(tile[0, chunk(m)], vec[t, 0], preferred_element_type=F32)
-            y = y + jnp.dot(tile[1, chunk(m)], vec[t, 1], preferred_element_type=F32)
-            sums[t, chunk(m)] = y
-
-            @pl.when(t > 0)
-            def _():
-                wait_partial(t, m)
-                sums[t, chunk(m)] = sums[t, chunk(m)] + partial[t, chunk(m)]
-
-            @pl.when(t == TICKS - 1)
-            def _():
-                tail[m * group:(m + 1) * group] = laid(sums[t, chunk(m)])
-
-            @pl.when((t < TICKS - 1) & jnp.logical_not(is_next))
-            def _():
-                partial_copy(t, m).start()
-
-            @pl.when((t < TICKS - 1) & is_next)
-            def _():
-                after = jnp.minimum(t + 1, TICKS - 1)
-                res[after, half, chunk(m)] = (given(after, m) - sums[t, chunk(m)]).astype(BF16)
-                res_copy(after, m).start()
-
-        @pl.when(is_next & (t < TICKS - 1))
-        def _():
-            @pl.when(t == 0)
-            def _():
-                for k in range(per):
-                    for h in range(2):
-                        @pl.when(half == h)
-                        def _():
-                            diag_copy(h, k).wait_recv()
-                    lay_diag(k)
-
-            solve(jnp.minimum(t + 1, TICKS - 1))
+        @pl.when(is_next)
+        def _():
+            after = jnp.minimum(t + 1, TICKS - 1)
+
+            @pl.when((t == 1) & moved)
+            def _():
+                wait_grad(2)
+
+            for m in range(CHUNKS):
+                @pl.when(t > 0)
+                def _():
+                    wait_sum(near, t, m, 1)
+
+                total = product(t, m) + near[t, chunk(m)].astype(F32)
+
+                @pl.when((t < TICKS - 1) & (apart | (t == 0)))
+                def _():
+                    first[after, chunk(m)] = total.astype(BF16)
+                    first_copy(after, m).start()
+
+                @pl.when((t > 0) & (t < TICKS - 1) & moved)
+                def _():
+                    res[after, half, chunk(m)] = (given(after, m) - total).astype(BF16)
+                    res_copy(after, m).start()
+
+                @pl.when(t == TICKS - 1)
+                def _():
+                    tail[m * group:(m + 1) * group] = laid(total)
+
+            @pl.when((t == 0) & moved)
+            def _():
+                lay_blocks(0, per // 2)
+
+            @pl.when((t == 1) & moved)
+            def _():
+                lay_blocks(per // 2, per)
+
+            @pl.when((t > 0) & (t < TICKS - 1) & moved)
+            def _():
+                solve(after)
+
+        @pl.when(jnp.logical_not(is_next))
+        def _():
+            for m in range(CHUNKS):
+                @pl.when(t > 0)
+                def _():
+                    wait_sum(partial, t, m, 0)
+
+                total = product(t, m) + partial[t, chunk(m)]
+
+                @pl.when((t < TICKS - 1) & into_next)
+                def _():
+                    near_sums[t, chunk(m)] = total.astype(BF16)
+                    near_sum(t, m).start()
+
+                @pl.when((t < TICKS - 1) & jnp.logical_not(into_next))
+                def _():
+                    sums[t, chunk(m)] = total
+                    far_sum(t, m).start()
+
+                @pl.when(t == TICKS - 1)
+                def _():
+                    tail[m * group:(m + 1) * group] = laid(total)
 
     @pl.loop(0, TICKS)
     def _(t):
-        @pl.when(is_next & (t == TICKS - 1))
-        def _():
-            @pl.loop(0, owners)
-            def _(o):
-                give(o, x_ret.at[rest, o], x_in.at[rest], rs_sem, r_sem.at[1])
+        @pl.when(is_next & moved & (t == TICKS - 1))
+        def _():
+            give_rest()
 
         @pl.when(is_lower & (blk >= t))
         def _():
@@ -335,7 +430,9 @@
         def _(o):
             give(o, tail.at[o], tail_in.at[slot], ts_sem, t_sem.at[slot])
 
-    pltpu.make_async_copy(x_in.at[0], x_in.at[0], r_sem.at[0]).wait()
+    @pl.when(jnp.logical_not(is_upper))
+    def _():
+        wait_start()
 
     @pl.when(row > 0)
     def _():
@@ -358,13 +455,18 @@
     for p in range(blocks):
         out_ref[:, p * width:(p + 1) * width] = grad_own[starts_ref[p]]
 
-    for k in range(2):
-        @pl.when(grad_goes[k] & (col != pieces[k][2]))
+    @pl.when(is_next & (blk == 0))
+    def _():
+        wait_grad(2)
+        lay_blocks(per // 2, per)
+
+    for k in range(3):
+        @pl.when(((row > 0) | (k < 2)) & (col != pieces[k][2]))
         def _():
             grad_copy(k).wait_send()
 
     for h in range(2):
-        @pl.when(is_diag & (row > 0) & (half == h))
+        @pl.when(is_diag & moved & (half == h))
         def _():
             for k in range(per):
                 diag_copy(h, k).wait_send()
@@ -376,14 +478,18 @@
     @pl.loop(0, TICKS)
     def _(t):
         for m in range(CHUNKS):
-            @pl.when((is_diag & (t == 0)) | (is_next & (t > 0) & (row >= t)))
+            @pl.when((row >= t) & ((is_diag & (apart | (t < 2))) | (is_next & moved & (t > 1))))
             def _():
                 res_copy(t, m).wait_send()
-                for k in (1, 2):
-                    @pl.when(row + k < blocks)
+                for k in range(2):
+                    @pl.when(row + 1 + k < blocks)
                     def _():
                         solved_copy(t, m, k).wait_send()
 
+            @pl.when(is_next & (row >= t) & ((t == 1) | (apart & (t > 0))))
+            def _():
+                first_copy(t, m).wait_send()
+
             @pl.when(is_lower & (blk >= t))
             def _():
                 vec_copy(t, m).wait_send()
@@ -392,9 +498,13 @@
                 def _():
                     forward_copy(t, m).wait_send()
 
-                @pl.when((t < TICKS - 1) & jnp.logical_not(is_next))
-                def _():
-                    partial_copy(t, m).wait_send()
+                @pl.when((t < TICKS - 1) & into_next)
+                def _():
+                    near_sum(t, m).wait_send()
+
+                @pl.when((t < TICKS - 1) & (row > blk + 2))
+                def _():
+                    far_sum(t, m).wait_send()
 
     def sent_all(ref_all, ref_less, sem):
         @pl.when(my_group == half)
@@ -413,11 +523,11 @@
 
     @pl.when(is_diag)
     def _():
-        sent_all(x_ret.at[0], x_ret.at[0, less], rs_sem)
-
-    @pl.when(is_next)
-    def _():
-        sent_all(x_ret.at[rest], x_ret.at[rest, less], rs_sem)
+        sent_all(x_ret.at[start], x_ret.at[start, less], rs_sem.at[0])
+
+    @pl.when((is_diag & apart & (row > 0)) | (is_next & moved))
+    def _():
+        sent_all(x_ret.at[rest], x_ret.at[rest, less], rs_sem.at[1])
 
 
 def body(factor, gradient, starts):
@@ -438,6 +548,10 @@
         vmem((TICKS, half_rows, width), BF16),
         vmem((TICKS, half_rows, width), F32),
         vmem((TICKS, half_rows, width), F32),
+        vmem((TICKS, half_rows, width), BF16),
+        vmem((TICKS, half_rows, width), BF16),
+        vmem((TICKS, half_rows, width), BF16),
+        vmem((TICKS, half_rows, width), BF16),
         vmem((owners, 64, width), BF16),
         vmem((blocks, rows, width), F32),
         vmem((blocks, rows, width), F32),
@@ -446,10 +560,10 @@
         vmem((TICKS, owners, 64, width), BF16),
         vmem((TICKS, 64, width), BF16),
         vmem((spare, 64, width), BF16),
-        dma, dma((2,)), dma((half_rows // 128,)), dma((half_rows // 128,)), dma((2,)), dma((2,)),
+        dma, dma((2,)), dma((half_rows // 128,)), dma((half_rows // 128,)), dma((3,)), dma((3,)),
         dma((2, TICKS, CHUNKS)), dma((2, TICKS, CHUNKS)), dma((2, TICKS, CHUNKS)),
-        dma((TICKS, CHUNKS)), dma((TICKS, CHUNKS)), dma((TICKS, CHUNKS)), dma((TICKS, CHUNKS)),
-        dma, dma((2,)), dma, dma((spare,)),
+        dma((TICKS, CHUNKS)), dma((TICKS, CHUNKS)), dma((2, TICKS, CHUNKS)), dma((2, TICKS, CHUNKS)),
+        dma((TICKS, CHUNKS)), dma((TICKS, CHUNKS)), dma((2,)), dma((2,)), dma, dma((spare,)),
     ]
     return pl.pallas_call(
         functools.partial(kernel, blocks),

time: 173 us -> 150 us (0.87)
  the two profiles are of different devices: /device:TPU:51 before, /device:TPU:63 now
where the time goes in v2:
time: 150 us
  Pallas kernels  148 us (99%)
  local copies, waits for them, and re-layouts  1.82 us (1%)
    pallas_call x1, Pallas kernels, body(): pl.pallas_call(functools.partial(kernel, blocks), out_shape=jax.ShapeDtyp...  148 us

profile of v2, /device:TPU:63, one launch (start us, length us, event | category | flops | bytes accessed | tf_op | source)
XLA Modules:
  0.0 150.1 jit_solution(12373027061496501672)
XLA Ops:
  0.0 148.3 %shard_map.37 = f32[56,2048]{1,0:T(8,128)} custom-call(s32[16]{0:T(128)} %starts_ref.1, f32[56,2048]{1,0:T(8,128)} %grad_ref.1, bf16[1792,896]{1,0:T(8,128)(2,1)} %factor_ref.1), custom_call_target="tpu_custom_call" | custom-call | flops 2466250752 | bytes 3211264 | tf_op jit(solution)/shard_map/pallas_call | solution.py:568
  148.3 1.8 %copy.5 = f32[56,2048]{1,0:T(8,128)} copy(f32[56,2048]{1,0:T(8,128)} %shard_map.37) | data formatting | bytes 917504

commit v3 on v2

--- a/solution.py
+++ b/solution.py
@@ -7,7 +7,10 @@
 from jax.sharding import PartitionSpec as P
 
 TICKS = 6
-CHUNKS = 2
+CHUNKS = 4
+FIRST = 3
+SINGLE = 3
+EARLY = 3
 MESH = pl.DeviceIdType.MESH
 F32 = jnp.float32
 BF16 = jnp.bfloat16
@@ -16,8 +19,8 @@
 def kernel(
     blocks, starts_ref, grad_ref, factor_ref, out_ref,
     tile, raw, diag, vec, res, solved, partial, sums, near, near_sums, first, first_in,
-    tail, grad_given, grad_own, grad_send, grad_in, x_ret, x_in, tail_in,
-    load_sem, tile_sem, us_sem, u_sem, gs_sem, g_sem, vs_sem, v_sem, xs_sem, qs_sem, q_sem,
+    tail, grad_all, grad_given, grad_own, grad_send, grad_in, x_ret, x_in, tail_in,
+    grad_sem, load_sem, tile_sem, us_sem, u_sem, gs_sem, g_sem, vs_sem, v_sem, xs_sem, qs_sem, q_sem,
     ss_sem, s_sem, fs_sem, f_sem, rs_sem, r_sem, ts_sem, t_sem,
 ):
     row = lax.axis_index("row")
@@ -37,9 +40,8 @@
     is_diag = row == blk
     is_next = row == blk + 1
     is_lower = row > blk
-    is_upper = row < blk
-    apart = row % 4 == 0
-    moved = jnp.logical_not(apart)
+    limit = jnp.where(row % 4 == 0, TICKS, FIRST)
+    moved = (row >= limit) & (limit < TICKS)
     my_group = col // owners
     diag_core = 2 * row + my_group
     next_core = jnp.where(row > 0, diag_core - 2, diag_core)
@@ -48,6 +50,9 @@
     other_rows = pl.ds(pl.multiple_of(other * half_rows, half_rows), half_rows)
     load_raw = pltpu.make_async_copy(factor_ref, raw, load_sem)
     load_half = pltpu.make_async_copy(factor_ref.at[own_rows], tile.at[half], load_sem)
+
+    load_grad = pltpu.make_async_copy(grad_ref, grad_all, grad_sem)
+    load_grad.start()
 
     @pl.when(is_diag)
     def _():
@@ -72,8 +77,9 @@
             device_id_type=MESH,
         )
 
+    load_grad.wait()
     for p in range(blocks):
-        grad_given[p] = grad_ref[:, p * width:(p + 1) * width]
+        grad_given[p] = grad_all[:, p * width:(p + 1) * width]
     for s in range(blocks):
         which = jnp.int32(0)
         for p in range(blocks):
@@ -94,42 +100,35 @@
     pl.semaphore_wait(barrier, 2 * blocks - 1 + len(far))
 
     my_slot = col % owners
-    pieces = ((0, 1, diag_core), (1, 1, diag_core), (2, TICKS - 2, jnp.where(apart, diag_core, next_core)))
-
-    def grad_copy(k):
-        lo, n, target = pieces[k]
+
+    def grad_target(t):
+        return jnp.where(t < limit, diag_core, next_core)
+
+    def grad_copy(t):
         return pltpu.make_async_remote_copy(
-            src_ref=grad_send.at[pl.ds(lo, n)],
-            dst_ref=grad_in.at[pl.ds(lo, n), my_slot],
-            send_sem=gs_sem.at[k], recv_sem=g_sem.at[k],
-            device_id=(row, target), device_id_type=MESH,
-        )
-
-    def grad_local(k):
-        lo, n, target = pieces[k]
-        return pltpu.make_async_copy(
-            grad_send.at[pl.ds(lo, n)], grad_in.at[pl.ds(lo, n), my_slot], g_sem.at[k]
-        )
-
-    def wait_grad(k):
-        lo, n, target = pieces[k]
-        pltpu.make_async_copy(grad_in.at[pl.ds(lo, n)], grad_in.at[pl.ds(lo, n)], g_sem.at[k]).wait()
-
-    def send_grad(k):
-        @pl.when(col != pieces[k][2])
-        def _():
-            grad_copy(k).start()
-
-        @pl.when(col == pieces[k][2])
-        def _():
-            grad_local(k).start()
+            src_ref=grad_send.at[t], dst_ref=grad_in.at[t, my_slot],
+            send_sem=gs_sem.at[t], recv_sem=g_sem.at[t],
+            device_id=(row, grad_target(t)), device_id_type=MESH,
+        )
+
+    def wait_grad(t):
+        pltpu.make_async_copy(grad_in.at[t], grad_in.at[t], g_sem.at[t]).wait()
+
+    def send_grad(t):
+        @pl.when((row >= t) & (col != grad_target(t)))
+        def _():
+            grad_copy(t).start()
+
+        @pl.when((row >= t) & (col == grad_target(t)))
+        def _():
+            pltpu.make_async_copy(grad_send.at[t], grad_in.at[t, my_slot], g_sem.at[t]).start()
+
+    def sent_grad(t):
+        @pl.when((row >= t) & (col != grad_target(t)))
+        def _():
+            grad_copy(t).wait_send()
 
     send_grad(0)
-    send_grad(1)
-
-    @pl.when(row > 0)
-    def _():
-        send_grad(2)
 
     def diag_copy(h, k):
         part = (pl.ds(0, h * half_rows + (k + 1) * lanes), pl.ds(k * lanes, lanes))
@@ -233,6 +232,22 @@
 
     def given(t, m):
         return grad_in[t, m * group:(m + 1) * group].astype(F32)[:, :rows].reshape(step, width)
+
+    def give(o, src, dst, send_sem, recv_sem):
+        target = half * owners + o
+
+        @pl.when(target != col)
+        def _():
+            pltpu.make_async_remote_copy(
+                src_ref=src, dst_ref=dst, send_sem=send_sem, recv_sem=recv_sem,
+                device_id=(row, target), device_id_type=MESH,
+            ).start()
+
+        @pl.when(target == col)
+        def _():
+            pltpu.make_async_copy(src, dst, recv_sem).start()
+
+    slot = jnp.clip(blk - (TICKS - 1), 0, tail_in.shape[0] - 1)
 
     def solve(t):
         for m in range(CHUNKS):
@@ -241,34 +256,30 @@
             x = jnp.dot(diag[0, chunk(m)], res[t, 0], preferred_element_type=F32)
             x = x + jnp.dot(diag[1, chunk(m)], res[t, 1], preferred_element_type=F32)
             solved[t, chunk(m)] = x.astype(BF16)
-            for k in range(2):
-                @pl.when(row + 1 + k < blocks)
-                def _():
-                    solved_copy(t, m, k).start()
             x_ret[t, m * group:(m + 1) * group] = laid(x)
 
-    def give(o, src, dst, send_sem, recv_sem):
-        target = half * owners + o
-
-        @pl.when(target != col)
-        def _():
-            pltpu.make_async_remote_copy(
-                src_ref=src, dst_ref=dst, send_sem=send_sem, recv_sem=recv_sem,
-                device_id=(row, target), device_id_type=MESH,
-            ).start()
-
-        @pl.when(target == col)
-        def _():
-            pltpu.make_async_copy(src, dst, recv_sem).start()
-
-    slot = jnp.clip(blk - (TICKS - 1), 0, tail_in.shape[0] - 1)
-    start = pl.ds(0, 2)
-    rest = pl.ds(2, TICKS - 2)
+            @pl.when(row + 1 < blocks)
+            def _():
+                solved_copy(t, m, 0).start()
+
+        @pl.when(row + 2 < blocks)
+        def _():
+            for m in range(CHUNKS):
+                solved_copy(t, m, 1).start()
+
+        @pl.when(t < SINGLE)
+        def _():
+            @pl.loop(0, owners)
+            def _(o):
+                give(o, x_ret.at[t, o], x_in.at[t], rs_sem.at[t], r_sem.at[t])
+
+    rest = pl.ds(SINGLE, TICKS - SINGLE)
+    rest_by_diag = limit == TICKS
 
     def give_rest():
         @pl.loop(0, owners)
         def _(o):
-            give(o, x_ret.at[rest, o], x_in.at[rest], rs_sem.at[1], r_sem.at[1])
+            give(o, x_ret.at[rest, o], x_in.at[rest], rs_sem.at[SINGLE], r_sem.at[SINGLE])
 
     def solve_apart(t):
         for m in range(CHUNKS):
@@ -282,31 +293,35 @@
         load_raw.wait()
         for k in range(per):
             lay_diag(k)
+
+    sent_grad(0)
+    send_grad(1)
+    sent_grad(1)
+    for t in range(2, EARLY):
+        send_grad(t)
+
+    def send_late():
+        for t in range(EARLY, TICKS):
+            send_grad(t)
+
+    @pl.when(is_diag)
+    def _():
         wait_grad(0)
         for m in range(CHUNKS):
             res[0, half, chunk(m)] = given(0, m).astype(BF16)
             res_copy(0, m).start()
         solve(0)
-        wait_grad(1)
-
-        @pl.when(row > 0)
-        def _():
-            solve_apart(1)
-
-        @pl.loop(0, owners)
-        def _(o):
-            give(o, x_ret.at[start, o], x_in.at[start], rs_sem.at[0], r_sem.at[0])
-
-        @pl.when(apart & (row > 0))
-        def _():
-            wait_grad(2)
-
-            @pl.loop(2, TICKS)
-            def _(t):
-                @pl.when(row >= t)
-                def _():
-                    solve_apart(t)
-
+        send_late()
+
+        @pl.loop(1, TICKS)
+        def _(t):
+            @pl.when((row >= t) & (t < limit))
+            def _():
+                wait_grad(t)
+                solve_apart(t)
+
+        @pl.when(rest_by_diag & (row >= SINGLE))
+        def _():
             give_rest()
 
     @pl.when(is_lower)
@@ -316,13 +331,6 @@
         load_half.wait()
         tile_copy.wait_recv()
 
-    def wait_start():
-        pltpu.make_async_copy(x_in.at[start], x_in.at[start], r_sem.at[0]).wait()
-
-    @pl.when(is_upper)
-    def _():
-        wait_start()
-
     def lay_blocks(lo, hi):
         for k in range(lo, hi):
             for h in range(2):
@@ -352,9 +360,11 @@
         def _():
             after = jnp.minimum(t + 1, TICKS - 1)
 
-            @pl.when((t == 1) & moved)
-            def _():
-                wait_grad(2)
+            fused = (t + 1 >= limit) & (t < TICKS - 1)
+
+            @pl.when(fused)
+            def _():
+                wait_grad(after)
 
             for m in range(CHUNKS):
                 @pl.when(t > 0)
@@ -363,12 +373,12 @@
 
                 total = product(t, m) + near[t, chunk(m)].astype(F32)
 
-                @pl.when((t < TICKS - 1) & (apart | (t == 0)))
+                @pl.when(t + 1 < limit)
                 def _():
                     first[after, chunk(m)] = total.astype(BF16)
                     first_copy(after, m).start()
 
-                @pl.when((t > 0) & (t < TICKS - 1) & moved)
+                @pl.when(fused)
                 def _():
                     res[after, half, chunk(m)] = (given(after, m) - total).astype(BF16)
                     res_copy(after, m).start()
@@ -377,15 +387,15 @@
                 def _():
                     tail[m * group:(m + 1) * group] = laid(total)
 
-            @pl.when((t == 0) & moved)
+            @pl.when((t == limit - 2) & moved)
             def _():
                 lay_blocks(0, per // 2)
 
-            @pl.when((t == 1) & moved)
+            @pl.when((t == limit - 1) & moved)
             def _():
                 lay_blocks(per // 2, per)
 
-            @pl.when((t > 0) & (t < TICKS - 1) & moved)
+            @pl.when(fused)
             def _():
                 solve(after)
 
@@ -412,9 +422,21 @@
                 def _():
                     tail[m * group:(m + 1) * group] = laid(total)
 
+    def wait_solved(t):
+        pltpu.make_async_copy(x_in.at[t], x_in.at[t], r_sem.at[t]).wait()
+
+    @pl.when(row < blk)
+    def _():
+        wait_solved(0)
+        send_late()
+
     @pl.loop(0, TICKS)
     def _(t):
-        @pl.when(is_next & moved & (t == TICKS - 1))
+        @pl.when(is_lower & (t == 1))
+        def _():
+            send_late()
+
+        @pl.when(is_next & (t == TICKS - 1) & (row >= SINGLE) & jnp.logical_not(rest_by_diag))
         def _():
             give_rest()
 
@@ -430,13 +452,15 @@
         def _(o):
             give(o, tail.at[o], tail_in.at[slot], ts_sem, t_sem.at[slot])
 
-    @pl.when(jnp.logical_not(is_upper))
-    def _():
-        wait_start()
-
-    @pl.when(row > 0)
-    def _():
-        pltpu.make_async_copy(x_in.at[rest], x_in.at[rest], r_sem.at[1]).wait()
+    @pl.loop(0, SINGLE)
+    def _(t):
+        @pl.when((row >= t) & ((t > 0) | (row >= blk)))
+        def _():
+            wait_solved(t)
+
+    @pl.when(row >= SINGLE)
+    def _():
+        pltpu.make_async_copy(x_in.at[rest], x_in.at[rest], r_sem.at[SINGLE]).wait()
 
     @pl.loop(0, blocks)
     def _(s):
@@ -455,15 +479,8 @@
     for p in range(blocks):
         out_ref[:, p * width:(p + 1) * width] = grad_own[starts_ref[p]]
 
-    @pl.when(is_next & (blk == 0))
-    def _():
-        wait_grad(2)
-        lay_blocks(per // 2, per)
-
-    for k in range(3):
-        @pl.when(((row > 0) | (k < 2)) & (col != pieces[k][2]))
-        def _():
-            grad_copy(k).wait_send()
+    for t in range(2, TICKS):
+        sent_grad(t)
 
     for h in range(2):
         @pl.when(is_diag & moved & (half == h))
@@ -478,7 +495,7 @@
     @pl.loop(0, TICKS)
     def _(t):
         for m in range(CHUNKS):
-            @pl.when((row >= t) & ((is_diag & (apart | (t < 2))) | (is_next & moved & (t > 1))))
+            @pl.when((row >= t) & ((is_diag & (t < limit)) | (is_next & (t >= limit))))
             def _():
                 res_copy(t, m).wait_send()
                 for k in range(2):
@@ -486,7 +503,7 @@
                     def _():
                         solved_copy(t, m, k).wait_send()
 
-            @pl.when(is_next & (row >= t) & ((t == 1) | (apart & (t > 0))))
+            @pl.when(is_next & (row >= t) & (t > 0) & (t < limit))
             def _():
                 first_copy(t, m).wait_send()
 
@@ -521,13 +538,15 @@
     def _():
         sent_all(tail, tail.at[less], ts_sem)
 
-    @pl.when(is_diag)
-    def _():
-        sent_all(x_ret.at[start], x_ret.at[start, less], rs_sem.at[0])
-
-    @pl.when((is_diag & apart & (row > 0)) | (is_next & moved))
-    def _():
-        sent_all(x_ret.at[rest], x_ret.at[rest, less], rs_sem.at[1])
+    @pl.loop(0, SINGLE)
+    def _(t):
+        @pl.when((row >= t) & ((is_diag & (t < limit)) | (is_next & (t >= limit))))
+        def _():
+            sent_all(x_ret.at[t], x_ret.at[t, less], rs_sem.at[t])
+
+    @pl.when((row >= SINGLE) & ((is_diag & rest_by_diag) | (is_next & jnp.logical_not(rest_by_diag))))
+    def _():
+        sent_all(x_ret.at[rest], x_ret.at[rest, less], rs_sem.at[SINGLE])
 
 
 def body(factor, gradient, starts):
@@ -553,6 +572,7 @@
         vmem((TICKS, half_rows, width), BF16),
         vmem((TICKS, half_rows, width), BF16),
         vmem((owners, 64, width), BF16),
+        vmem(gradient.shape, F32),
         vmem((blocks, rows, width), F32),
         vmem((blocks, rows, width), F32),
         vmem((TICKS, 64, width), BF16),
@@ -560,17 +580,17 @@
         vmem((TICKS, owners, 64, width), BF16),
         vmem((TICKS, 64, width), BF16),
         vmem((spare, 64, width), BF16),
-        dma, dma((2,)), dma((half_rows // 128,)), dma((half_rows // 128,)), dma((3,)), dma((3,)),
+        dma, dma, dma((2,)), dma((half_rows // 128,)), dma((half_rows // 128,)), dma((TICKS,)), dma((TICKS,)),
         dma((2, TICKS, CHUNKS)), dma((2, TICKS, CHUNKS)), dma((2, TICKS, CHUNKS)),
         dma((TICKS, CHUNKS)), dma((TICKS, CHUNKS)), dma((2, TICKS, CHUNKS)), dma((2, TICKS, CHUNKS)),
-        dma((TICKS, CHUNKS)), dma((TICKS, CHUNKS)), dma((2,)), dma((2,)), dma, dma((spare,)),
+        dma((TICKS, CHUNKS)), dma((TICKS, CHUNKS)), dma((TICKS,)), dma((TICKS,)), dma, dma((spare,)),
     ]
     return pl.pallas_call(
         functools.partial(kernel, blocks),
         out_shape=jax.ShapeDtypeStruct(gradient.shape, F32),
         in_specs=[
             pl.BlockSpec(memory_space=pltpu.SMEM),
-            pl.BlockSpec(memory_space=pltpu.VMEM),
+            pl.BlockSpec(memory_space=pl.ANY),
             pl.BlockSpec(memory_space=pl.ANY),
         ],
         out_specs=pl.BlockSpec(memory_space=pltpu.VMEM),

time: 150 us -> 146 us (0.973)
  Pallas kernels: 148 us -> 144 us
    pallas_call x1, Pallas kernels: 148 us -> 144 us  [body(): pl.pallas_call(functools.partial(kernel, blocks), out_shape=jax.ShapeDtyp...]
where the time goes in v3:
time: 146 us
  Pallas kernels  144 us (99%)
  local copies, waits for them, and re-layouts  1.82 us (1%)
    pallas_call x1, Pallas kernels, body(): pl.pallas_call(functools.partial(kernel, blocks), out_shape=jax.ShapeDtyp...  144 us

profile of v3, /device:TPU:63, one launch (start us, length us, event | category | flops | bytes accessed | tf_op | source)
XLA Modules:
  0.0 145.9 jit_solution(11760567606424331004)
XLA Ops:
  0.0 144.1 %shard_map.37 = f32[56,2048]{1,0:T(8,128)} custom-call(s32[16]{0:T(128)} %starts_ref.1, f32[56,2048]{1,0:T(8,128)} %grad_ref.1, bf16[1792,896]{1,0:T(8,128)(2,1)} %factor_ref.1), custom_call_target="tpu_custom_call" | custom-call | flops 2466250752 | bytes 3211264 | tf_op jit(solution)/shard_map/pallas_call | solution.py:588
  144.1 1.8 %copy.5 = f32[56,2048]{1,0:T(8,128)} copy(f32[56,2048]{1,0:T(8,128)} %shard_map.37) | data formatting | bytes 917504

commit v4 on v3

--- a/solution.py
+++ b/solution.py
@@ -19,7 +19,7 @@
 def kernel(
     blocks, starts_ref, grad_ref, factor_ref, out_ref,
     tile, raw, diag, vec, res, solved, partial, sums, near, near_sums, first, first_in,
-    tail, grad_all, grad_given, grad_own, grad_send, grad_in, x_ret, x_in, tail_in,
+    own_part, tail, grad_all, grad_given, grad_own, grad_send, grad_in, x_ret, x_in, tail_in,
     grad_sem, load_sem, tile_sem, us_sem, u_sem, gs_sem, g_sem, vs_sem, v_sem, xs_sem, qs_sem, q_sem,
     ss_sem, s_sem, fs_sem, f_sem, rs_sem, r_sem, ts_sem, t_sem,
 ):
@@ -251,16 +251,18 @@
 
     def solve(t):
         for m in range(CHUNKS):
+            own_part[chunk(m)] = jnp.dot(diag[half, chunk(m)], res[t, half], preferred_element_type=F32)
+        for m in range(CHUNKS):
             res_copy(t, m).wait_recv()
         for m in range(CHUNKS):
-            x = jnp.dot(diag[0, chunk(m)], res[t, 0], preferred_element_type=F32)
-            x = x + jnp.dot(diag[1, chunk(m)], res[t, 1], preferred_element_type=F32)
+            x = own_part[chunk(m)] + jnp.dot(diag[other, chunk(m)], res[t, other], preferred_element_type=F32)
             solved[t, chunk(m)] = x.astype(BF16)
+
+            @pl.when(row + 1 < blocks)
+            def _():
+                solved_copy(t, m, 0).start()
+
             x_ret[t, m * group:(m + 1) * group] = laid(x)
-
-            @pl.when(row + 1 < blocks)
-            def _():
-                solved_copy(t, m, 0).start()
 
         @pl.when(row + 2 < blocks)
         def _():
@@ -340,18 +342,20 @@
             lay_diag(k)
 
     def product(t, m):
-        y = jnp.dot(tile[0, chunk(m)], vec[t, 0], preferred_element_type=F32)
-        return y + jnp.dot(tile[1, chunk(m)], vec[t, 1], preferred_element_type=F32)
+        return own_part[chunk(m)] + jnp.dot(tile[other, chunk(m)], vec[t, other], preferred_element_type=F32)
 
     def tick(t):
         for m in range(CHUNKS):
             forward_copy(t, m).wait_recv()
 
+            vec_copy(t, m).start()
+
             @pl.when(row + 2 < blocks)
             def _():
                 forward_copy(t, m).start()
 
-            vec_copy(t, m).start()
+        for m in range(CHUNKS):
+            own_part[chunk(m)] = jnp.dot(tile[half, chunk(m)], vec[t, half], preferred_element_type=F32)
 
         for m in range(CHUNKS):
             vec_copy(t, m).wait_recv()
@@ -571,6 +575,7 @@
         vmem((TICKS, half_rows, width), BF16),
         vmem((TICKS, half_rows, width), BF16),
         vmem((TICKS, half_rows, width), BF16),
+        vmem((half_rows, width), F32),
         vmem((owners, 64, width), BF16),
         vmem(gradient.shape, F32),
         vmem((blocks, rows, width), F32),

time: 146 us -> 146 us (level)
  no operation moved by 1% of the time
where the time goes in v4:
time: 146 us; the launch traced here: 145 us
  Pallas kernels  144 us (99%)
  local copies, waits for them, and re-layouts  1.82 us (1%)
    pallas_call x1, Pallas kernels, body(): pl.pallas_call(functools.partial(kernel, blocks), out_shape=jax.ShapeDtyp...  144 us

profile of v4, /device:TPU:63, one launch (start us, length us, event | category | flops | bytes accessed | tf_op | source)
XLA Modules:
  0.0 145.4 jit_solution(13179526965162118364)
XLA Ops:
  0.0 143.6 %shard_map.37 = f32[56,2048]{1,0:T(8,128)} custom-call(s32[16]{0:T(128)} %starts_ref.1, f32[56,2048]{1,0:T(8,128)} %grad_ref.1, bf16[1792,896]{1,0:T(8,128)(2,1)} %factor_ref.1), custom_call_target="tpu_custom_call" | custom-call | flops 2466250752 | bytes 3211264 | tf_op jit(solution)/shard_map/pallas_call | solution.py:593
  143.6 1.8 %copy.5 = f32[56,2048]{1,0:T(8,128)} copy(f32[56,2048]{1,0:T(8,128)} %shard_map.37) | data formatting | bytes 917504
